TPU v7x, 512 devices: a whole 4x4x16 slice. The times are simulated.
512 devices in a mesh: tok: 32 (over z, core), wid: 16 (over y, x).
Axes of the slice: x: 4, y: 4, z: 16, core: 2. Of those that a mesh axis runs over, the one named last changes fastest.
Arguments:
- hidden: bfloat16 [16896, 1280], P('tok', 'wid'), may hold values from -30 to 30
- w_qkv: bfloat16 [1280, 1920], P('tok', 'wid'), may hold values from -0.15625 to 0.15625
- w_out: bfloat16 [1280, 1280], P('tok', 'wid'), may hold values from -0.15625 to 0.15625
- w_gate: bfloat16 [1280, 3584], P('tok', 'wid'), may hold values from -0.15625 to 0.15625
- w_up: bfloat16 [1280, 3584], P('tok', 'wid'), may hold values from -0.15625 to 0.15625
- w_down: bfloat16 [3584, 1280], P('wid', 'tok'), may hold values from -0.1875 to 0.1875
- g_attn: float32 [1280], replicated, may hold values from 0.1 to 1.9
- g_ffn: float32 [1280], replicated, may hold values from 0.1 to 1.9
- lengths: int32 [544], P('tok'), may hold values from 0 to 2048, as said below
- k_cache: bfloat16 [544, 2048, 320], P('tok', 'wid'), may hold values from -45 to 45
- v_cache: bfloat16 [544, 2048, 320], P('tok', 'wid'), may hold values from -4 to 4
Outputs:
- output: bfloat16 [16896, 1280], P('tok', 'wid')
- new_kv: bfloat16 [16896, 640], P('tok', 'wid')
Inputs may be any that keep to these rules, and one draw needn't show every extreme that they name: `lengths`: each request's entry is at most 2048, and some request has exactly 2048.
All inputs are finite; a program needn't handle non-finite values.
Results may differ from a plain program's by a relative error of at most 0.017.
Values may be sent and summed in bfloat16 or wider, within the bound.
No kernel may reach another device: no remote copies, remote signals or barrier semaphores. Data moves between devices by JAX's collectives and lax.ppermute only.
A program may use at most 64 MiB of HBM per device.

v0:
```python
import jax
import jax.numpy as jnp
from jax import lax
from jax.sharding import PartitionSpec as P

HEADS = 20
KV_HEADS = 5
HEAD_DIM = 64
STRETCH = 512
EPSILON = 1e-05
MASKED = -1e30
SCORE_SCALE = 0.125


def norm_rows(values, gain):
    wide = values.astype(jnp.float32)
    mean_square = jnp.mean(wide * wide, axis=-1, keepdims=True)
    return (wide * lax.rsqrt(mean_square + EPSILON) * gain).astype(jnp.bfloat16)


def rotate(parts, places):
    half = parts.shape[-1] // 2
    ladder = jnp.arange(half).astype(jnp.float32) * (2.0 / parts.shape[-1])
    freqs = jnp.power(10000.0, -ladder)
    angles = places.astype(jnp.float32)[:, None] * freqs[None, :]
    cosine = jnp.cos(angles)[:, None, :]
    sine = jnp.sin(angles)[:, None, :]
    first = parts[..., :half]
    second = parts[..., half:]
    return jnp.concatenate(
        [first * cosine - second * sine, second * cosine + first * sine], axis=-1
    )


def shards(hidden, w_qkv, w_out, w_gate, w_up, w_down, g_attn, g_ffn, lengths, k_cache, v_cache):
    wid_count = lax.axis_size("wid")
    wid_place = lax.axis_index("wid")
    row_count = hidden.shape[0]
    query_width = HEADS * HEAD_DIM
    kv_width = KV_HEADS * HEAD_DIM
    groups = HEADS // KV_HEADS
    full_rows = lax.all_gather(hidden, "wid", axis=1, tiled=True)
    normed = norm_rows(full_rows, g_attn)
    tall_cols = lax.all_gather(w_qkv, "tok", axis=0, tiled=True)
    own_cols = jnp.dot(normed, tall_cols, preferred_element_type=jnp.float32)
    mixed = lax.all_gather(own_cols.astype(jnp.bfloat16), "wid", axis=1, tiled=True)
    stretch_rows = lengths[0] + jnp.arange(STRETCH)
    places = jnp.concatenate([stretch_rows, lengths[1:]])
    query = rotate(
        mixed[:, :query_width].astype(jnp.float32).reshape(row_count, HEADS, HEAD_DIM), places
    ).astype(jnp.bfloat16)
    keys = rotate(
        mixed[:, query_width : query_width + kv_width]
        .astype(jnp.float32)
        .reshape(row_count, KV_HEADS, HEAD_DIM),
        places,
    ).astype(jnp.bfloat16)
    values = mixed[:, query_width + kv_width :]
    new_kv_all = jnp.concatenate([keys.reshape(row_count, kv_width), values], axis=1)
    kv_share = 2 * kv_width // wid_count
    new_kv = lax.dynamic_slice_in_dim(new_kv_all, wid_place * kv_share, kv_share, 1)
    value_heads = values.reshape(row_count, KV_HEADS, HEAD_DIM)
    span = k_cache.shape[1]
    requests = k_cache.shape[0]
    query_heads = query.reshape(row_count, KV_HEADS, groups, HEAD_DIM)
    old_keys = k_cache.reshape(requests, span, KV_HEADS, HEAD_DIM)
    old_values = v_cache.reshape(requests, span, KV_HEADS, HEAD_DIM)
    spots = wid_place * span + jnp.arange(span)
    live = spots[None, :] < lengths[:, None]
    score_stretch = (
        jnp.einsum(
            "rkgd,pkd->rkgp", query_heads[:STRETCH], old_keys[0], preferred_element_type=jnp.float32
        )
        * SCORE_SCALE
    )
    score_stretch = jnp.where(live[0][None, None, None, :], score_stretch, MASKED)
    score_decode = (
        jnp.einsum(
            "jkgd,jpkd->jkgp",
            query_heads[STRETCH:],
            old_keys[1:],
            preferred_element_type=jnp.float32,
        )
        * SCORE_SCALE
    )
    score_decode = jnp.where(live[1:][:, None, None, :], score_decode, MASKED)
    band = row_count // wid_count
    first_row = wid_place * band
    query_mine = lax.dynamic_slice_in_dim(query_heads, first_row, band, 0)
    later = first_row + jnp.arange(band)[:, None]
    earlier = jnp.arange(row_count)[None, :]
    fresh_ok = (later < STRETCH) & (earlier < STRETCH) & (earlier <= later) | (later >= STRETCH) & (
        earlier == later
    )
    score_fresh = (
        jnp.einsum("rkgd,jkd->rkgj", query_mine, keys, preferred_element_type=jnp.float32)
        * SCORE_SCALE
    )
    score_fresh = jnp.where(fresh_ok[:, None, None, :], score_fresh, MASKED)
    cache_peak = jnp.concatenate([score_stretch.max(-1), score_decode.max(-1)], axis=0)
    fresh_peak = lax.dynamic_update_slice_in_dim(
        jnp.full(cache_peak.shape, MASKED, jnp.float32), score_fresh.max(-1), first_row, 0
    )
    peak = lax.pmax(jnp.maximum(cache_peak, fresh_peak).astype(jnp.bfloat16), "wid").astype(
        jnp.float32
    )
    expo_stretch = jnp.exp(score_stretch - peak[:STRETCH, :, :, None])
    expo_decode = jnp.exp(score_decode - peak[STRETCH:, :, :, None])
    peak_mine = lax.dynamic_slice_in_dim(peak, first_row, band, 0)
    expo_fresh = jnp.exp(score_fresh - peak_mine[:, :, :, None])
    totals = jnp.concatenate([expo_stretch.sum(-1), expo_decode.sum(-1)], axis=0)
    sums = jnp.concatenate(
        [
            jnp.einsum(
                "rkgp,pkd->rkgd",
                expo_stretch.astype(jnp.bfloat16),
                old_values[0],
                preferred_element_type=jnp.float32,
            ),
            jnp.einsum(
                "jkgp,jpkd->jkgd",
                expo_decode.astype(jnp.bfloat16),
                old_values[1:],
                preferred_element_type=jnp.float32,
            ),
        ],
        axis=0,
    )
    fresh_sums = jnp.einsum(
        "rkgj,jkd->rkgd",
        expo_fresh.astype(jnp.bfloat16),
        value_heads,
        preferred_element_type=jnp.float32,
    )
    sums = lax.dynamic_update_slice_in_dim(
        sums, lax.dynamic_slice_in_dim(sums, first_row, band, 0) + fresh_sums, first_row, 0
    )
    totals = lax.dynamic_update_slice_in_dim(
        totals,
        lax.dynamic_slice_in_dim(totals, first_row, band, 0) + expo_fresh.sum(-1),
        first_row,
        0,
    )
    sums_all, totals_all = (
        lax.psum(sums.reshape(row_count, query_width).astype(jnp.bfloat16), "wid").astype(
            jnp.float32
        ),
        lax.psum(totals.reshape(row_count, HEADS).astype(jnp.bfloat16), "wid").astype(jnp.float32),
    )
    merged = sums_all.reshape(row_count, HEADS, HEAD_DIM) / totals_all[:, :, None]
    attended = merged.astype(jnp.bfloat16).reshape(row_count, query_width)
    out_whole = lax.all_gather(w_out, "tok", axis=0, tiled=True)
    projected = jnp.dot(attended, out_whole, preferred_element_type=jnp.float32)
    residual = hidden.astype(jnp.float32) + projected
    middle = residual.astype(jnp.bfloat16)
    middle_full = lax.all_gather(middle, "wid", axis=1, tiled=True)
    normed_ffn = norm_rows(middle_full, g_ffn)
    gate_whole, up_whole = (
        lax.all_gather(w_gate, "tok", axis=0, tiled=True),
        lax.all_gather(w_up, "tok", axis=0, tiled=True),
    )
    gate = jnp.dot(normed_ffn, gate_whole, preferred_element_type=jnp.float32)
    up = jnp.dot(normed_ffn, up_whole, preferred_element_type=jnp.float32)
    activated = (jax.nn.silu(gate) * up).astype(jnp.bfloat16)
    down_full = lax.all_gather(w_down, "tok", axis=1, tiled=True)
    own_sums = lax.psum_scatter(
        lax.dot_general(
            down_full, activated, (((0,), (1,)), ((), ())), preferred_element_type=jnp.float32
        ).astype(jnp.bfloat16),
        "wid",
        scatter_dimension=0,
        tiled=True,
    ).astype(jnp.float32)
    output = (residual + own_sums.T).astype(jnp.bfloat16)
    return (output, new_kv)


def solution(mesh):
    placed = (
        P("tok", "wid"),
        P("tok", "wid"),
        P("tok", "wid"),
        P("tok", "wid"),
        P("tok", "wid"),
        P("wid", "tok"),
        P(),
        P(),
        P("tok"),
        P("tok", "wid", None),
        P("tok", "wid", None),
    )
    return jax.shard_map(
        shards,
        mesh=mesh,
        in_specs=placed,
        out_specs=(P("tok", "wid"), P("tok", "wid")),
        check_vma=False,
    )
```

profile of v0, /device:TPU:2, one launch (start us, length us, event | category | flops | bytes accessed | tf_op | source)
XLA Modules:
  0.0 582.2 jit_solution(18248502710288355273)
XLA Ops:
  7.2 0.7 all-gather.5.cloned.1.call-update
  8.0 37.4 %all_gather.25 = bf16[1280,120]{1,0:T(8,128)(2,1)S(1)} all-gather(bf16[40,120]{1,0:T(8,128)(2,1)} %param.12), channel_id=1, replica_groups=mesh['tok'=32,'wid'=16] {'tok'}, dimensions={0}, use_global_device_ids=true | all-gather | bytes 316800 | tf_op jit(solution)/shard_map/all_gather | solution.py:44
  45.3 29.2 %all-gather.5.cloned.1.call-done = bf16[528,1280]{0,1:T(8,128)(2,1)} async-done(((bf16[528,80]{0,1:T(8,128)(2,1)}), bf16[528,1280]{0,1:T(8,128)(2,1)}) %all-gather.5.cloned.1.call-update) | async-done | bytes 1351696 | tf_op jit(solution)/shard_map/all_gather | solution.py:42
  74.5 1.8 fusion.3
  76.4 3.0 fusion.33
  79.4 1.3 copy-done.5
  80.7 0.6 slice.89
  81.3 1.2 slice.91
  82.8 0.5 slice_bitcast_fusion
  83.3 0.1 fusion.57
  83.4 0.4 multiply_cosine_fusion
  83.8 55.9 %all-gather.9.cloned.1.call-done = bf16[16,120,528]{1,2,0:T(8,128)(2,1)} async-done(((bf16[1,120,528]{1,2,0:T(8,128)(2,1)}), bf16[16,120,528]{1,2,0:T(8,128)(2,1)}) %all-gather.9.cloned.1.call-update) | async-done | bytes 2027536 | tf_op jit(solution)/shard_map/all_gather | solution.py:46
  139.7 2.2 copy.52
  141.8 3.6 reshape.238
  145.4 1.5 slice_convert_fusion
  147.0 2.5 fusion.70
  149.4 2.4 copy.53
  151.8 2.4 subtract_convert_fusion
  154.2 2.7 copy.58
  156.8 2.6 copy.59
  159.5 1.2 fusion.26
  160.7 0.1 pad_maximum_fusion.1
  160.8 1.6 copy.57
  162.3 0.9 multiply_subtract_fusion
  163.2 0.2 copy.55
  163.4 1.1 fusion.72
  164.5 0.1 copy.56
  164.6 2.0 fusion.71
  166.7 0.9 dynamic_update_slice.9
  167.6 3.3 bitcast_reduce_fusion
  170.9 67.5 %pmax.7 = bf16[528,5,4]{0,2,1:T(4,128)(2,1)S(1)} all-reduce(bf16[528,5,4]{0,2,1:T(4,128)(2,1)S(1)} %fusion.62), channel_id=1, replica_groups=mesh['tok'=32,'wid'=16] {'wid'}, use_global_device_ids=true, to_apply=%region_4.5 | all-reduce | flops 10560 | bytes 42240 | tf_op jit(solution)/shard_map/pmax | solution.py:104
  238.4 0.6 slice.104
  239.1 0.1 copy.61
  239.2 0.6 copy-done.9
  239.9 2.2 fusion.59
  242.1 0.3 copy.62
  242.4 0.2 copy.63
  242.6 3.9 fusion.19
  246.5 1.5 pad_maximum_fusion
  248.0 1.9 fusion.27
  249.9 6.7 %dynamic_update_slice.10 = bf16[528,5,4,64]{0,3,2,1:T(8,128)(2,1)} dynamic-update-slice(bf16[528,5,4,64]{0,3,2,1:T(8,128)(2,1)} %pad_maximum_fusion, bf16[33,5,4,64]{0,3,2,1:T(8,128)(2,1)} %fusion.27, s32[]{:T(128)S(6)} %select_n.30, s32[]{:T(128)} %constant.11.clone.1, s32[]{:T(128)} %constant.11.clone.1, s32[]{:T(128)} %constant.11.clone.1) | dynamic-update-slice | bytes 168964 | tf_op jit(solution)/shard_map/dynamic_update_slice | solution.py:135
  256.7 31.9 %all_gather.27 = bf16[1280,80]{1,0:T(8,128)(2,1)S(1)} all-gather(bf16[40,80]{1,0:T(8,128)(2,1)S(1)} %copy-done.14), channel_id=1, replica_groups=mesh['tok'=32,'wid'=16] {'tok'}, dimensions={0}, use_global_device_ids=true | all-gather | bytes 211200 | tf_op jit(solution)/shard_map/all_gather | solution.py:152
  288.6 0.3 fusion.54
  288.9 0.1 copy.65
  289.0 3.7 fusion.1
  292.7 0.6 fusion.17
  293.3 0.1 fusion.64
  293.4 0.9 dynamic_update_slice.11
  294.3 69.2 %psum.15 = bf16[528,20]{0,1:T(8,128)(2,1)S(1)} all-reduce(bf16[528,20]{0,1:T(8,128)(2,1)S(1)} %convert_element_type.114), channel_id=1, replica_groups=mesh['tok'=32,'wid'=16] {'wid'}, use_global_device_ids=true, to_apply=%region_9.10 | all-reduce | flops 10560 | bytes 42240 | tf_op jit(solution)/shard_map/psum | solution.py:148
  363.5 12.9 %all-reduce.3.cloned.1.call-done = bf16[528,1280]{0,1:T(8,128)(2,1)} async-done(((bf16[528,1280]{0,1:T(8,128)(2,1)}), bf16[528,1280]{0,1:T(8,128)(2,1)}) %all-reduce.3.cloned.1.call-update) | async-done | bytes 1351696 | tf_op jit(solution)/shard_map/psum | solution.py:145
  376.3 1.8 fusion.9
  378.1 1.1 fusion.73
  379.3 35.5 %all_gather.29 = bf16[1280,224]{1,0:T(8,128)(2,1)} all-gather(bf16[40,224]{1,0:T(8,128)(2,1)S(1)} %copy-done.11), channel_id=1, replica_groups=mesh['tok'=32,'wid'=16] {'tok'}, dimensions={0}, use_global_device_ids=true | all-gather | bytes 591360 | tf_op jit(solution)/shard_map/all_gather | solution.py:159
  414.8 29.9 %all_gather.30 = bf16[1280,224]{1,0:T(8,128)(2,1)S(1)} all-gather(bf16[40,224]{1,0:T(8,128)(2,1)S(1)} %copy-done.12), channel_id=1, replica_groups=mesh['tok'=32,'wid'=16] {'tok'}, dimensions={0}, use_global_device_ids=true | all-gather | bytes 591360 | tf_op jit(solution)/shard_map/all_gather | solution.py:160
  444.6 33.2 %all_gather.31 = bf16[224,1280]{0,1:T(8,128)(2,1)} all-gather(bf16[224,40]{0,1:T(8,128)(2,1)S(1)} %copy-done.13), channel_id=1, replica_groups=mesh['tok'=32,'wid'=16] {'tok'}, dimensions={1}, use_global_device_ids=true | all-gather | bytes 591360 | tf_op jit(solution)/shard_map/all_gather | solution.py:165
  477.9 1.8 fusion.6
  479.8 3.4 fusion.46
  483.2 4.1 fusion.10
  487.2 2.7 copy.66
  490.0 0.2 copy.67
  490.3 0.2 fusion.53
  490.5 0.7 copy.68
  491.2 82.9 %reduce-scatter.4.cloned.1.call-done = bf16[80,528]{1,0:T(8,128)(2,1)} async-done(((bf16[1280,528]{1,0:T(8,128)(2,1)}), bf16[80,528]{1,0:T(8,128)(2,1)}) %reduce-scatter.4.cloned.1.call-update) | async-done | bytes 84496
  574.1 1.6 fusion.52
  (71 shorter events, 0.8 us)
Async XLA Ops:
  7.2 69.2 %copy-start.17 = (f32[1280]{0:T(1024)S(1)}, f32[1280]{0:T(1024)}, u32[]{:S(2)}) copy-start(f32[1280]{0:T(1024)} %param.17) | copy-start | bytes 15364
  7.2 67.4 %all-gather.5.cloned.1.call-start = ((), (), s32[]{:S(2)}) async-start(), calls=%async_computation.1 | async-start | bytes 1740800 | tf_op jit(solution)/shard_map/all_gather | solution.py:42
  7.9 131.8 %all-gather.9.cloned.1.call-start = ((), (), s32[]{:S(2)}) async-start(), calls=%async_computation.4 | async-start | bytes 2297856 | tf_op jit(solution)/shard_map/all_gather | solution.py:46
  79.3 1.3 copy-start.5
  79.4 297.0 %all-reduce.3.cloned.1.call-start = ((), (), s32[]{:S(2)}) async-start(), calls=%async_computation.2 | async-start | bytes 3276800 | tf_op jit(solution)/shard_map/psum | solution.py:145
  80.7 1.8 copy-start.16
  160.8 2.6 slice-start.1
  164.6 2.9 slice-start
  164.6 2.9 copy-start
  164.6 3.0 copy-start.15
  170.9 71.5 %copy-start.1 = (bf16[528,320]{1,0:T(8,128)(2,1)S(1)}, bf16[528,320]{1,0:T(8,128)(2,1)}, u32[]{:S(2)}) copy-start(bf16[528,320]{1,0:T(8,128)(2,1)} %get-tuple-element.10) | copy-start | bytes 1013764
  239.2 0.6 copy-start.9
  249.9 6.8 %copy-start.14 = (bf16[40,80]{1,0:T(8,128)(2,1)S(1)}, bf16[40,80]{1,0:T(8,128)(2,1)}, u32[]{:S(2)}) copy-start(bf16[40,80]{1,0:T(8,128)(2,1)} %param.13) | copy-start | bytes 19204
  249.9 38.7 %copy-start.6 = (f32[16,5,4,128]{3,2,1,0:T(4,128)S(1)}, f32[16,5,4,128]{3,2,1,0:T(4,128)}, u32[]{:S(2)}) copy-start(f32[16,5,4,128]{3,2,1,0:T(4,128)} %get-tuple-element.19) | copy-start | bytes 491524
  249.9 38.7 %copy-start.10 = (f32[16,5,4]{2,1,0:T(8,128)S(1)}, f32[16,5,4]{2,1,0:T(8,128)}, u32[]{:S(2)}) copy-start(f32[16,5,4]{2,1,0:T(8,128)} %copy-done.9) | copy-start | bytes 3844
  249.9 39.1 %copy-start.8 = (f32[512,5,4]{0,2,1:T(4,128)S(1)}, f32[512,5,4]{0,2,1:T(4,128)}, u32[]{:S(2)}) copy-start(f32[512,5,4]{0,2,1:T(4,128)} %slice.104) | copy-start | bytes 122884
  256.6 221.3 %all-gather.7.cloned.1.call-start = ((), (), s32[]{:S(2)}) async-start(), calls=%async_computation.3 | async-start | bytes 1740800 | tf_op jit(solution)/shard_map/all_gather | solution.py:156
  293.3 84.8 %copy-start.7 = (bf16[528,80]{0,1:T(8,128)(2,1)S(1)}, bf16[528,80]{0,1:T(8,128)(2,1)}, u32[]{:S(2)}) copy-start(bf16[528,80]{0,1:T(8,128)(2,1)} %param.11) | copy-start | bytes 253444
  378.1 1.2 copy-start.11
  378.1 36.7 %copy-start.12 = (bf16[40,224]{1,0:T(8,128)(2,1)S(1)}, bf16[40,224]{1,0:T(8,128)(2,1)}, u32[]{:S(2)}) copy-start(bf16[40,224]{1,0:T(8,128)(2,1)} %param.15) | copy-start | bytes 53764
  378.1 66.5 %copy-start.13 = (bf16[224,40]{0,1:T(8,128)(2,1)S(1)}, bf16[224,40]{0,1:T(8,128)(2,1)}, u32[]{:S(2)}) copy-start(bf16[224,40]{0,1:T(8,128)(2,1)} %param.16) | copy-start | bytes 53764
  379.2 100.5 %copy-start.18 = (f32[1280]{0:T(1024)S(1)}, f32[1280]{0:T(1024)}, u32[]{:S(2)}) copy-start(f32[1280]{0:T(1024)} %param.18) | copy-start | bytes 15364
  379.3 194.8 %reduce-scatter.4.cloned.1.call-start = ((), (), s32[]{:S(2)}) async-start(), calls=%async_computation.5 | async-start | bytes 1740800
  479.7 3.4 copy-start.4
  487.2 2.7 copy-start.2
  487.2 2.7 copy-start.3
Sparse Core Ops, SparseCore 0:
  11.0 63.4 all-gather.4
  79.5 60.1 all-gather.8
  256.7 119.5 all-reduce.2
  379.8 58.7 all-gather.6
  490.1 83.9 reduce-scatter.3
where the time goes:
time: 583 us; the launch traced here: 582 us
  blocking collectives  305 us (52%)
  waiting for transfers between devices  182 us (31%)
  local copies, waits for them, and re-layouts  33.2 us (6%)
  matrix products  25.9 us (4%)
  other arithmetic  22.6 us (4%)
  between operations  14.2 us (2%)
    unnamed x6, waiting for transfers between devices  83.6 us
    psum x1, blocking collectives, shards(): lax.psum(totals.reshape(row_count, HEADS).astype(jnp.bfloat16), 'wid')  69.2 us
    pmax x1, blocking collectives, shards(): lax.pmax(jnp.maximum(cache_peak, fresh_peak).astype(jnp.bfloat16), 'wid')  67.5 us
    all_gather x1, waiting for transfers between devices, shards(): lax.all_gather(own_cols.astype(jnp.bfloat16), 'wid', axis=1, tiled=True)  55.9 us
    all_gather x1, blocking collectives, shards(): tall_cols = lax.all_gather(w_qkv, 'tok', axis=0, tiled=True)  37.4 us
    all_gather x1, blocking collectives, shards(): lax.all_gather(w_gate, 'tok', axis=0, tiled=True)  35.5 us
    all_gather x1, blocking collectives, shards(): down_full = lax.all_gather(w_down, 'tok', axis=1, tiled=True)  33.2 us
    all_gather x1, blocking collectives, shards(): out_whole = lax.all_gather(w_out, 'tok', axis=0, tiled=True)  31.9 us
  transfers between devices with their start and end apart: 5, of which 4 were waited for; matrix products, arithmetic and copies ran while one was open for 2% of the time, Pallas kernels for 0%

commit v1 on v0

--- a/solution.py
+++ b/solution.py
@@ -10,6 +10,10 @@
 EPSILON = 1e-05
 MASKED = -1e30
 SCORE_SCALE = 0.125
+
+
+def reach_column_up(x_local):
+    return jnp.sum(lax.all_gather(x_local, "wid"), axis=0)
 
 
 def norm_rows(values, gain):
@@ -142,7 +146,7 @@
         0,
     )
     sums_all, totals_all = (
-        lax.psum(sums.reshape(row_count, query_width).astype(jnp.bfloat16), "wid").astype(
+        reach_column_up(sums.reshape(row_count, query_width).astype(jnp.bfloat16)).astype(
             jnp.float32
         ),
         lax.psum(totals.reshape(row_count, HEADS).astype(jnp.bfloat16), "wid").astype(jnp.float32),

time: 583 us -> 629 us (1.079)
  waiting for transfers between devices: 182 us -> 208 us
  other arithmetic: 22.6 us -> 32.3 us
    all_gather x0 -> x1, waiting for transfers between devices: none -> 39.1 us  [reach_column_up(): return jnp.sum(lax.all_gather(x_local, 'wid'), axis=0)]
    psum x1 -> x0, waiting for transfers between devices: 12.9 us -> none  [shards(): lax.psum(sums.reshape(row_count, query_width).astype(jnp.bfloat16), 'wid')]
    reduce_sum x0 -> x1, other arithmetic: none -> 12.6 us  [reach_column_up(): return jnp.sum(lax.all_gather(x_local, 'wid'), axis=0)]
where the time goes in v1:
time: 629 us; the launch traced here: 628 us
  blocking collectives  308 us (49%)
  waiting for transfers between devices  208 us (33%)
  local copies, waits for them, and re-layouts  39.4 us (6%)
  other arithmetic  32.3 us (5%)
  matrix products  25.7 us (4%)
  between operations  14.2 us (2%)
    unnamed x6, waiting for transfers between devices  83.5 us
    psum x1, blocking collectives, shards(): lax.psum(totals.reshape(row_count, HEADS).astype(jnp.bfloat16), 'wid')  70.1 us
    pmax x1, blocking collectives, shards(): lax.pmax(jnp.maximum(cache_peak, fresh_peak).astype(jnp.bfloat16), 'wid')  67.3 us
    all_gather x1, waiting for transfers between devices, shards(): lax.all_gather(own_cols.astype(jnp.bfloat16), 'wid', axis=1, tiled=True)  56.6 us
    all_gather x1, waiting for transfers between devices, reach_column_up(): return jnp.sum(lax.all_gather(x_local, 'wid'), axis=0)  39.1 us
    all_gather x1, blocking collectives, shards(): tall_cols = lax.all_gather(w_qkv, 'tok', axis=0, tiled=True)  37.4 us
    all_gather x1, blocking collectives, shards(): out_whole = lax.all_gather(w_out, 'tok', axis=0, tiled=True)  34.6 us
    all_gather x1, blocking collectives, shards(): down_full = lax.all_gather(w_down, 'tok', axis=1, tiled=True)  33.2 us
  transfers between devices with their start and end apart: 5, of which 4 were waited for; matrix products, arithmetic and copies ran while one was open for 2% of the time, Pallas kernels for 0%

profile of v1, /device:TPU:2, one launch (start us, length us, event | category | flops | bytes accessed | tf_op | source)
XLA Modules:
  0.0 628.1 jit_solution(15950542224097528934)
XLA Ops:
  7.2 0.7 all-gather.6.cloned.1.call-update
  8.0 37.4 %all_gather.29 = bf16[1280,120]{1,0:T(8,128)(2,1)S(1)} all-gather(bf16[40,120]{1,0:T(8,128)(2,1)} %param.12), channel_id=1, replica_groups=mesh['tok'=32,'wid'=16] {'tok'}, dimensions={0}, use_global_device_ids=true | all-gather | bytes 316800 | tf_op jit(solution)/shard_map/all_gather | solution.py:48
  45.3 29.2 %all-gather.6.cloned.1.call-done = bf16[528,1280]{0,1:T(8,128)(2,1)} async-done(((bf16[528,80]{0,1:T(8,128)(2,1)}), bf16[528,1280]{0,1:T(8,128)(2,1)}) %all-gather.6.cloned.1.call-update) | async-done | bytes 1351696 | tf_op jit(solution)/shard_map/all_gather | solution.py:46
  74.5 1.8 fusion.3
  76.4 3.0 fusion.34
  79.4 1.3 copy-done.8
  80.7 1.2 slice.91
  82.1 0.5 slice_bitcast_fusion
  82.7 0.4 multiply_cosine_fusion
  83.1 56.6 %all-gather.12.cloned.1.call-done = bf16[16,120,528]{1,2,0:T(8,128)(2,1)} async-done(((bf16[1,120,528]{1,2,0:T(8,128)(2,1)}), bf16[16,120,528]{1,2,0:T(8,128)(2,1)}) %all-gather.12.cloned.1.call-update) | async-done | bytes 2027536 | tf_op jit(solution)/shard_map/all_gather | solution.py:50
  139.7 3.5 copy.70
  143.2 3.9 reshape.249
  147.0 1.3 copy-done
  148.3 1.2 fusion.71
  149.6 1.5 slice_convert_fusion
  151.1 2.4 copy.71
  153.5 2.4 subtract_convert_fusion
  156.0 1.2 fusion.26
  157.2 2.6 copy.77
  159.8 2.6 copy.76
  162.4 0.3 copy.75
  162.8 0.9 multiply_subtract_fusion
  163.6 0.2 copy.73
  163.8 1.1 fusion.73
  164.9 0.1 copy.74
  165.1 2.0 fusion.72
  167.1 0.9 dynamic_update_slice.9
  168.0 3.3 bitcast_reduce_fusion
  171.4 67.3 %pmax.7 = bf16[528,5,4]{0,2,1:T(4,128)(2,1)S(1)} all-reduce(bf16[528,5,4]{0,2,1:T(4,128)(2,1)S(1)} %fusion.63), channel_id=1, replica_groups=mesh['tok'=32,'wid'=16] {'wid'}, use_global_device_ids=true, to_apply=%region_4.5 | all-reduce | flops 10560 | bytes 42240 | tf_op jit(solution)/shard_map/pmax | solution.py:108
  238.8 1.2 copy.81
  240.0 0.7 constant_dynamic-slice_fusion
  240.7 0.1 copy.79
  240.8 2.3 fusion.60
  243.1 0.3 copy.80
  243.3 3.9 fusion.18
  247.2 1.5 pad_maximum_fusion
  248.7 1.1 fusion.27
  249.8 6.6 %dynamic_update_slice.10 = bf16[528,5,4,64]{0,3,2,1:T(8,128)(2,1)} dynamic-update-slice(bf16[528,5,4,64]{0,3,2,1:T(8,128)(2,1)} %pad_maximum_fusion, bf16[33,5,4,64]{0,3,2,1:T(8,128)(2,1)S(1)} %fusion.27, s32[]{:T(128)S(6)} %select_n.30, s32[]{:T(128)} %constant.13.clone.1, s32[]{:T(128)} %constant.13.clone.1, s32[]{:T(128)} %constant.13.clone.1) | dynamic-update-slice | bytes 168964 | tf_op jit(solution)/shard_map/dynamic_update_slice | solution.py:139
  256.4 2.7 copy.83
  259.2 34.6 %all_gather.32 = bf16[1280,80]{1,0:T(8,128)(2,1)} all-gather(bf16[40,80]{1,0:T(8,128)(2,1)S(1)} %copy-done.17), channel_id=1, replica_groups=mesh['tok'=32,'wid'=16] {'tok'}, dimensions={0}, use_global_device_ids=true | all-gather | bytes 211200 | tf_op jit(solution)/shard_map/all_gather | solution.py:156
  293.8 0.3 fusion.55
  294.1 0.1 copy.84
  294.2 3.8 fusion.1
  298.0 0.6 fusion.16
  298.7 0.9 dynamic_update_slice.11
  299.6 70.1 %psum.7 = bf16[528,20]{0,1:T(8,128)(2,1)S(1)} all-reduce(bf16[528,20]{0,1:T(8,128)(2,1)S(1)} %convert_element_type.125), channel_id=1, replica_groups=mesh['tok'=32,'wid'=16] {'wid'}, use_global_device_ids=true, to_apply=%region_9.10 | all-reduce | flops 10560 | bytes 42240 | tf_op jit(solution)/shard_map/psum | solution.py:152
  369.7 0.2 div.22
  369.9 2.3 copy.85
  372.3 39.1 %all-gather.8.cloned.1.call-done = bf16[16,528,1280]{2,1,0:T(8,128)(2,1)} async-done(((bf16[1,528,1280]{2,1,0:T(8,128)(2,1)}), bf16[16,528,1280]{2,1,0:T(8,128)(2,1)}) %all-gather.8.cloned.1.call-update) | async-done | bytes 21626896 | tf_op jit(solution)/shard_map/all_gather | solution.py:16
  411.4 12.6 %reduce_sum.58 = bf16[528,1280]{1,0:T(8,128)(2,1)} reduce(bf16[16,528,1280]{2,1,0:T(8,128)(2,1)} %all-gather.8.cloned.1.call-done, bf16[]{:T(256)} %constant.15.clone.1), dimensions={0}, to_apply=%region_5.6 | reduce | flops 10137600 | bytes 22978562 | tf_op jit(solution)/shard_map/reduce_sum | solution.py:16
  424.0 2.6 fusion.74
  426.7 32.8 %all_gather.34 = bf16[1280,224]{1,0:T(8,128)(2,1)S(1)} all-gather(bf16[40,224]{1,0:T(8,128)(2,1)S(1)} %copy-done.14), channel_id=1, replica_groups=mesh['tok'=32,'wid'=16] {'tok'}, dimensions={0}, use_global_device_ids=true | all-gather | bytes 591360 | tf_op jit(solution)/shard_map/all_gather | solution.py:163
  459.5 32.5 %all_gather.35 = bf16[1280,224]{1,0:T(8,128)(2,1)} all-gather(bf16[40,224]{1,0:T(8,128)(2,1)S(1)} %copy-done.15), channel_id=1, replica_groups=mesh['tok'=32,'wid'=16] {'tok'}, dimensions={0}, use_global_device_ids=true | all-gather | bytes 591360 | tf_op jit(solution)/shard_map/all_gather | solution.py:164
  492.0 33.2 %all_gather.36 = bf16[224,1280]{0,1:T(8,128)(2,1)} all-gather(bf16[224,40]{0,1:T(8,128)(2,1)S(1)} %copy-done.16), channel_id=1, replica_groups=mesh['tok'=32,'wid'=16] {'tok'}, dimensions={1}, use_global_device_ids=true | all-gather | bytes 591360 | tf_op jit(solution)/shard_map/all_gather | solution.py:169
  525.2 1.8 fusion.6
  527.1 3.3 fusion.47
  530.4 3.2 fusion.9
  533.6 1.7 copy.86
  535.3 0.2 copy.87
  535.6 0.7 copy-done.2
  536.3 0.2 fusion.54
  536.5 0.7 copy.88
  537.2 82.8 %reduce-scatter.4.cloned.1.call-done = bf16[80,528]{1,0:T(8,128)(2,1)} async-done(((bf16[1280,528]{1,0:T(8,128)(2,1)}), bf16[80,528]{1,0:T(8,128)(2,1)}) %reduce-scatter.4.cloned.1.call-update) | async-done | bytes 84496
  620.0 1.6 fusion.53
  (80 shorter events, 1.0 us)
Async XLA Ops:
  7.2 69.2 %copy-start.20 = (f32[1280]{0:T(1024)S(1)}, f32[1280]{0:T(1024)}, u32[]{:S(2)}) copy-start(f32[1280]{0:T(1024)} %param.17) | copy-start | bytes 15364
  7.2 67.4 %all-gather.6.cloned.1.call-start = ((), (), s32[]{:S(2)}) async-start(), calls=%async_computation.1 | async-start | bytes 1740800 | tf_op jit(solution)/shard_map/all_gather | solution.py:46
  7.9 131.8 %all-gather.12.cloned.1.call-start = ((), (), s32[]{:S(2)}) async-start(), calls=%async_computation.4 | async-start | bytes 2297856 | tf_op jit(solution)/shard_map/all_gather | solution.py:50
  79.3 1.3 copy-start.8
  79.4 332.0 %all-gather.8.cloned.1.call-start = ((), (), s32[]{:S(2)}) async-start(), calls=%async_computation.2 | async-start | bytes 22978560 | tf_op jit(solution)/shard_map/all_gather | solution.py:16
  79.4 2.4 copy-start.19
  147.0 1.3 copy-start
  159.8 2.6 copy-start.3
  162.4 1.4 slice-start.1
  165.1 2.9 slice-start
  165.1 2.9 copy-start.1
  165.1 3.0 copy-start.18
  171.4 72.0 %slice-start.2 = ((bf16[17,128,320]{1,2,0:T(8,128)(2,1)}), bf16[1,128,320]{1,2,0:T(8,128)(2,1)S(1)}, s32[]{:S(2)}) async-start(bf16[17,128,320]{1,2,0:T(8,128)(2,1)} %param.21), calls=%async_computation.8 | async-start | bytes 163840 | tf_op jit(solution)/shard_map/slice | solution.py:121
  247.2 1.5 copy-start.12
  256.4 2.7 copy-start.17
  256.4 37.3 %copy-start.9 = (f32[16,5,4,128]{3,2,1,0:T(4,128)S(1)}, f32[16,5,4,128]{3,2,1,0:T(4,128)}, u32[]{:S(2)}) copy-start(f32[16,5,4,128]{3,2,1,0:T(4,128)} %get-tuple-element.21) | copy-start | bytes 491524
  259.1 266.1 %all-gather.10.cloned.1.call-start = ((), (), s32[]{:S(2)}) async-start(), calls=%async_computation.3 | async-start | bytes 1740800 | tf_op jit(solution)/shard_map/all_gather | solution.py:160
  294.2 3.8 copy-start.13
  372.3 51.7 %copy-start.4 = (f32[528,1280]{1,0:T(8,128)S(1)}, f32[528,1280]{1,0:T(8,128)}, u32[]{:S(2)}) copy-start(f32[528,1280]{1,0:T(8,128)} %copy.85) | copy-start | bytes 8110084
  372.3 51.7 %copy-start.10 = (bf16[1280,80]{1,0:T(8,128)(2,1)S(1)}, bf16[1280,80]{1,0:T(8,128)(2,1)}, u32[]{:S(2)}) copy-start(bf16[1280,80]{1,0:T(8,128)(2,1)} %all_gather.32) | copy-start | bytes 614404
  372.3 51.7 %copy-start.11 = (bf16[528,80]{0,1:T(8,128)(2,1)S(1)}, bf16[528,80]{0,1:T(8,128)(2,1)}, u32[]{:S(2)}) copy-start(bf16[528,80]{0,1:T(8,128)(2,1)} %param.11) | copy-start | bytes 253444
  424.0 2.7 copy-start.14
  424.0 35.5 %copy-start.15 = (bf16[40,224]{1,0:T(8,128)(2,1)S(1)}, bf16[40,224]{1,0:T(8,128)(2,1)}, u32[]{:S(2)}) copy-start(bf16[40,224]{1,0:T(8,128)(2,1)} %param.15) | copy-start | bytes 53764
  424.0 68.0 %copy-start.16 = (bf16[224,40]{0,1:T(8,128)(2,1)S(1)}, bf16[224,40]{0,1:T(8,128)(2,1)}, u32[]{:S(2)}) copy-start(bf16[224,40]{0,1:T(8,128)(2,1)} %param.16) | copy-start | bytes 53764
  426.6 100.5 %copy-start.21 = (f32[1280]{0:T(1024)S(1)}, f32[1280]{0:T(1024)}, u32[]{:S(2)}) copy-start(f32[1280]{0:T(1024)} %param.18) | copy-start | bytes 15364
  426.6 193.4 %reduce-scatter.4.cloned.1.call-start = ((), (), s32[]{:S(2)}) async-start(), calls=%async_computation.5 | async-start | bytes 1740800
  527.1 3.3 copy-start.7
  533.5 1.7 copy-start.5
  533.5 1.7 copy-start.6
  535.3 1.0 copy-start.2
Sparse Core Ops, SparseCore 0:
  11.0 63.4 all-gather.5
  79.5 60.1 all-gather.11
  259.3 152.0 all-gather.7
  426.7 59.4 all-gather.9
  535.4 84.5 reduce-scatter.3
